TPU v7x, 128 devices: a whole 4x4x4 slice. The times are simulated.
128 devices in a mesh: section: 2 (over y_lo), dp: 16 (over x, y_hi, core), tensor: 4 (over z).
Axes of the slice: x: 4, y: 4 (y_hi: 2, y_lo: 2; y = y_hi * 2 + y_lo), z: 4, core: 2. Of those that a mesh axis runs over, the one named last changes fastest.
Arguments:
- series: float32 [512, 512], P('dp'), may hold values from -6 to 6
- missing: int32 [512, 512], P('dp'), may hold values 0 or 1
- w_in: bfloat16 [64, 1280], P(None, 'tensor'), may hold values from -0.75 to 0.75
- w_hid: bfloat16 [1280, 1280], P('tensor'), may hold values from -0.15625 to 0.15625
- w_res: bfloat16 [64, 1280], replicated, may hold values from -0.75 to 0.75
- gain_attn: float32 [2, 1280], P('section'), may hold values from 0.5 to 1.5
- w_qkv: bfloat16 [2, 1280, 3, 1280], P('section', None, None, 'tensor'), may hold values from -0.15625 to 0.15625
- w_out: bfloat16 [2, 1280, 1280], P('section', 'tensor'), may hold values from -0.5 to 0.5
- gain_mlp: float32 [2, 1280], P('section'), may hold values from 0.5 to 1.5
- w_up: bfloat16 [2, 1280, 5120], P('section', None, 'tensor'), may hold values from -0.15625 to 0.15625
- w_down: bfloat16 [2, 5120, 1280], P('section', 'tensor'), may hold values from -0.125 to 0.125
- cotangent: bfloat16 [8192, 1280], P('dp'), may hold values from -6 to 6
Outputs:
- layer_outputs: bfloat16 [2, 8192, 1280], P('section', 'dp')
- series_grad: float32 [512, 512], P('dp', ('section', 'tensor'))
- w_in_grad: float32 [64, 1280], P('section', 'tensor')
- w_hid_grad: float32 [1280, 1280], P('tensor', 'section')
- w_res_grad: float32 [64, 1280], P(None, 'section')
- gain_attn_grad: float32 [2, 1280], P('section')
- w_qkv_grad: float32 [2, 1280, 3, 1280], P('section', None, None, 'tensor')
- w_out_grad: float32 [2, 1280, 1280], P('section', 'tensor')
- gain_mlp_grad: float32 [2, 1280], P('section')
- w_up_grad: float32 [2, 1280, 5120], P('section', None, 'tensor')
- w_down_grad: float32 [2, 5120, 1280], P('section', 'tensor')
All inputs are finite; a program needn't handle non-finite values. No bound on the sum of `missing` on one device may be relied on, other than what follows from the above.
Results may differ from a plain program's by a relative error of at most 0.035.
Values may be sent and summed in bfloat16 or wider, within the bound.
A program may use at most 192 MiB of HBM per device.

v0:
```python
import math

import jax
import jax.numpy as jnp
import numpy as np
from jax import lax
from jax.experimental import pallas as pl
from jax.experimental.pallas import tpu as pltpu
from jax.sharding import PartitionSpec as P

D = 1280
HEADS_HERE = 4
HEAD_DIM = 80
ATT = HEADS_HERE * HEAD_DIM
PATCH = 32
PATCHES = 16
ROWS = 256
HALVES = 2
RH = ROWS // HALVES
RQ = RH // 4
TILE = 256
BLOCK = 128
MATS = ((0, 960), (960, 320), (1280, 1280), (2560, 1280))
PIECES = tuple((320 * i, 320, 0 if i < 3 else 1 if i < 4 else 2 if i < 8 else 3) for i in range(12))
N_PIECES = len(PIECES)
LAYER_ROWS = 3840
PACK_ROWS = 4096
RS_BEFORE = {2: 0, 3: 1, 5: 3, 6: 2, 7: 5, 8: 6, 4: 8}
MESH = pl.DeviceIdType.MESH
f32 = jnp.float32
bf16 = jnp.bfloat16
eps_norm = 1e-06
masked_score = -1e30
GELU_A = math.sqrt(2.0 / math.pi)
GELU_B = 0.044715


def mm(a, b):
    return lax.dot_general(a, b, (((1,), (0,)), ((), ())), preferred_element_type=f32)


def mm_t(a, b):
    return lax.dot_general(a, b, (((1,), (1,)), ((), ())), preferred_element_type=f32)


def tm(a, b):
    return lax.dot_general(a, b, (((0,), (0,)), ((), ())), preferred_element_type=f32)


def unrolled(count, body):
    for j in range(count):
        body(j, 0)


def rotary_arrays():
    half = HEAD_DIM // 2
    position = (np.arange(BLOCK) % PATCHES).astype(np.float32)
    frequency = np.exp(
        np.arange(half, dtype=np.float32) * np.float32(-2.0 * math.log(10000.0) / HEAD_DIM)
    )
    angles = position[:, None] * frequency[None, :]
    lane = np.arange(ATT) % half
    turn = np.zeros((ATT, ATT), np.float32)
    for j in range(ATT):
        if j % HEAD_DIM < half:
            turn[j + half, j] = -1.0
        else:
            turn[j - half, j] = 1.0
    return np.cos(angles)[:, lane], np.sin(angles)[:, lane], turn


def places():
    s = lax.axis_index("section")
    dp = lax.axis_index("dp")
    z = lax.axis_index("tensor")
    c = lax.rem(dp, 2)
    yh = lax.rem(lax.div(dp, 2), 2)
    x = lax.div(dp, 4)
    return s, dp, z, x, yh, c


def layers_kernel(
    series_ref, missing_ref, w_in_in, w_hid_in, w_res_in, gain_a_ref, gain_m_ref, wq_ref, wo_ref, wu_ref, wd_ref,
    cot_ref, cos_in, sin_in, turn_in,
    lo_ref, go_ref, points_ref,
    w_in_ref, w_hid_ref, w_res_ref, cos_ref, sin_ref, turn_ref, in_l,
    patch_ref, wb, gn, tokh, pre, sx, mid, nb, nm, qb, pb, ct, upb, hb, gb, mb, du, dqb, dctx, gv, gt,
    sb, rb, dmid, ob, gg, ggr, dps, dpr, gpad,
    th, r1, r2, ra1, ra2, rb3, tt, tx, ty, pd,
    w_loc, w_s, w_r, x_s, x_r, f_s, f_r, gn_s, gn_r, cot_l,
    rs_s, rs_r, ag_s, ag_r, lo_l, lo_s, lo_r, gg_s, gg_r, dp_s, dp_r,
    e_s, e_r, e_l, t_s, t_r, t_l, free_th, free_r1, free_r2,
):
    s, dp, z, x, yh, c = places()
    other = 1 - s
    z_peer = [None] + [(s, dp, lax.rem(z + d, 4)) for d in (1, 2, 3)]
    z_at = [z] + [lax.rem(z + d, 4) for d in (1, 2, 3)]
    y_a = (other, dp, z)
    y_b = (other, dp + 2 - 4 * yh, z)
    core = (s, dp + 1 - 2 * c, z)
    across = [(other, dp, z_at[d]) for d in range(4)]
    y = 2 * yh + s
    x_at = [x] + [lax.rem(x + d, 4) for d in (1, 2, 3)]
    y_at = [y] + [lax.rem(y + d, 4) for d in (1, 2, 3)]
    x_peer = [None] + [(s, x_at[d] * 4 + 2 * yh + c, z) for d in (1, 2, 3)]
    y_peer = [None] + [
        (lax.rem(y_at[d], 2), x * 4 + 2 * lax.div(y_at[d], 2) + c, z) for d in (1, 2, 3)
    ]
    x_up, x_down = x_peer[1], x_peer[3]
    w_refs = (wq_ref, wo_ref, wu_ref, wd_ref)

    small_inputs = [
        pltpu.make_async_copy(src, dst, in_l.at[i])
        for i, (src, dst) in enumerate((
            (w_in_in, w_in_ref), (w_hid_in, w_hid_ref), (w_res_in, w_res_ref),
            (cos_in, cos_ref), (sin_in, sin_ref), (turn_in, turn_ref),
        ))
    ]
    for copy in small_inputs:
        copy.start()
    barrier = pltpu.get_barrier_semaphore()
    peers = z_peer[1:] + across + [y_b, core] + x_peer[1:] + [y_peer[2]]
    for peer in peers:
        pl.semaphore_signal(barrier, inc=1, device_id=peer, device_id_type=MESH)
    pl.semaphore_wait(barrier, len(peers))

    def remote(src, dst, ssem, rsem, peer):
        return pltpu.make_async_remote_copy(
            src_ref=src, dst_ref=dst, send_sem=ssem, recv_sem=rsem,
            device_id=peer, device_id_type=MESH,
        )

    odd = lax.rem(x, 2)

    def w_local(m):
        off, n = MATS[m]
        return pltpu.make_async_copy(w_refs[m], wb.at[s, pl.ds(off, n)], w_loc)

    def share(i, parity, k):
        off, n, m = PIECES[i]
        first = (n // 4 + 31) // 32 * 16 if i % 2 == 0 else n // 4 // 32 * 16
        size = first if k == 0 else n // 4 - first
        return (2 * c + parity) * (n // 4) + k * first, size

    def w_over_y(i, k):
        off, n, m = PIECES[i]
        at, size = share(i, odd, k)
        src = w_refs[m].at[pl.ds(pl.multiple_of(off - MATS[m][0] + at, 16), size)]
        dst = wb.at[s, pl.ds(pl.multiple_of(off + at, 16), size)]
        return remote(src, dst, w_s, w_r.at[i], (y_a, y_b)[k])

    def w_over_x(i, k, parity):
        at, size = share(i, parity, k)
        ref = wb.at[other, pl.ds(pl.multiple_of(PIECES[i][0] + at, 16), size)]
        return remote(ref, ref, x_s, x_r.at[i], (x_up, x_down)[k])

    def w_to_core(i, q):
        off, n, m = PIECES[i]
        parity = odd if q == 0 else 1 - odd
        ref = wb.at[other, pl.ds(pl.multiple_of(off + (2 * c + parity) * (n // 4), 16), n // 4)]
        return remote(ref, ref, f_s, f_r.at[i], core)

    def w_total(i, part, ssem, rsem):
        ref = wb.at[0, pl.ds(0, PIECES[i][1] // part)]
        return remote(ref, ref, ssem, rsem.at[i], core)

    def w_sent(part, ssem, rsem):
        ref = wb.at[0, pl.ds(0, LAYER_ROWS // part)]
        return remote(ref, ref, ssem, rsem.at[0], core)

    def weights(layer, steps):
        @pl.when(s != layer)
        def _():
            for step, i in steps:
                if step == "y":
                    w_total(i, 4, w_s, w_r).wait_recv()
                    for k in range(2):
                        w_over_x(i, k, odd).start()
                    w_to_core(i, 0).start()
                elif step == "x":
                    w_total(i, 4, x_s, x_r).wait_recv()
                    w_to_core(i, 1).start()
                else:
                    w_total(i, 2, f_s, f_r).wait_recv()

    gains = gn.at[s]
    gains[0:1, :] = gain_a_ref[...]
    gains[1:2, :] = gain_m_ref[...]
    gn_send = remote(gn.at[s], gn.at[s], gn_s, gn_r, y_a)
    cot_copy = pltpu.make_async_copy(
        cot_ref.at[pl.ds(pl.multiple_of(s * ROWS, ROWS), ROWS)], gb.at[0], cot_l
    )
    gn_send.start()
    def start_weights(first, last):
        for i in range(first, last):
            for k in range(2):
                w_over_y(i, k).start()

    start_weights(0, 4)
    for m in range(4):
        w_local(m).start()
    cot_copy.start()

    def rows_of(h):
        return pl.ds(h * RH, RH)

    def chunk(h, zz):
        return pl.ds(pl.multiple_of(h * RH + zz * RQ, RQ), RQ)

    def cols_of(j):
        return pl.ds(j * TILE, TILE)

    def rs_copy(st, h, d, cols=None):
        src = sb.at[st % 2, chunk(h, z_at[d])]
        dst = rb.at[st % 2, d - 1, pl.ds(h * RQ, RQ)]
        if cols is not None:
            src = sb.at[st % 2, chunk(h, z_at[d]), cols]
            dst = rb.at[st % 2, d - 1, pl.ds(h * RQ, RQ), cols]
        return remote(src, dst, rs_s.at[st, h], rs_r.at[st, h], z_peer[d])

    def rs_total(st, h):
        ref = rb.at[st % 2, pl.ds(0, 3), pl.ds(h * RQ, RQ)]
        return remote(ref, ref, rs_s.at[st, h], rs_r.at[st, h], core)

    def rs_send(st, h, produce):
        if st in RS_BEFORE:
            rs_total(RS_BEFORE[st], h).wait_send()

        if produce is None:
            sb[st % 2, rows_of(h), :] = pd[rows_of(h), :]
            for d in (2, 1, 3):
                rs_copy(st, h, d).start()
            return

        def body(j, carry):
            cols = cols_of(j)
            sb[st % 2, rows_of(h), cols] = produce(j, cols).astype(bf16)
            if j in (2, 4):
                part = pl.ds(0, 768) if j == 2 else pl.ds(768, 512)
                for d in (2, 1, 3):
                    rs_copy(st, h, d, part).start()

        unrolled(D // TILE, body)

    def rs_take(st, h):
        total = sb[st % 2, chunk(h, z), :].astype(f32)
        rs_total(st, h).wait_recv()
        for d in (1, 2, 3):
            total = total + rb[st % 2, d - 1, pl.ds(h * RQ, RQ), :].astype(f32)
        return total

    def ag_copy(st, h, d, dst):
        at = dst.at[chunk(h, z)]
        return remote(at, at, ag_s.at[st, h], ag_r.at[st, h], z_peer[d])

    def ag_send(st, h, dst, value):
        dst[chunk(h, z), :] = value.astype(bf16)
        for d in (2, 1, 3):
            ag_copy(st, h, d, dst).start()

    def ag_total(st, h):
        ref = pd.at[pl.ds(0, 3 * RQ)]
        return remote(ref, ref, ag_s.at[st, h], ag_r.at[st, h], core)

    def ag_wait(st, h, dst):
        ag_total(st, h).wait_recv()

    def own(h):
        return pl.ds(h * RQ, RQ)

    def scale_of(v):
        return lax.rsqrt(jnp.mean(v * v, axis=-1, keepdims=True) + eps_norm)

    def norm(v, g):
        return v * scale_of(v) * g

    def norm_back(dn, v, g):
        r = scale_of(v)
        weighted = g * dn
        inner = jnp.mean(v * weighted, axis=-1, keepdims=True)
        return r * weighted - v * (r * r * r * inner), jnp.sum(dn * v * r, axis=0, keepdims=True)

    head_lane = lax.broadcasted_iota(jnp.int32, (1, ATT), 1)
    head_mask = [
        (head_lane >= HEAD_DIM * h) & (head_lane < HEAD_DIM * (h + 1)) for h in range(HEADS_HERE)
    ]

    def spread(v):
        wide = v.astype(f32)
        return jnp.concatenate(
            [jnp.where(m, wide, 0.0) for m in head_mask], axis=0
        ).astype(bf16)

    def gather(v):
        total = jnp.where(head_mask[0], v[:BLOCK], 0.0)
        for h in range(1, HEADS_HERE):
            total = total + jnp.where(head_mask[h], v[h * BLOCK : (h + 1) * BLOCK], 0.0)
        return total

    def turned(v, sign):
        high = v.astype(bf16)
        low = (v - high.astype(f32)).astype(bf16)
        swapped = mm(high, turn_ref[...]) + mm(low, turn_ref[...])
        if sign < 0:
            swapped = -swapped
        return v * cos_ref[...] + swapped * sin_ref[...]

    inv = 1.0 / math.sqrt(HEAD_DIM)

    def blocks_of(h):
        return range(h * RH // BLOCK, (h + 1) * RH // BLOCK)

    def attention_front(layer, h):
        for b in blocks_of(h):
            at = pl.ds(b * BLOCK, BLOCK)
            normed = nb[layer, at, :]
            first = b == 0
            if first:
                weights(layer, [("core", 0)])
            q = turned(mm_t(normed, wb[layer, 0:ATT, :]), 1).astype(bf16)
            if first:
                weights(layer, [("core", 1)])
            k = turned(mm_t(normed, wb[layer, ATT : 2 * ATT, :]), 1).astype(bf16)
            if first:
                weights(layer, [("core", 2)])
            v = mm_t(normed, wb[layer, 2 * ATT : 3 * ATT, :]).astype(bf16)
            qb[layer, 0, at, :] = q
            qb[layer, 1, at, :] = k
            qb[layer, 2, at, :] = v
            scores = mm_t(spread(q), k) * inv
            row = lax.broadcasted_iota(jnp.int32, scores.shape, 0) & (BLOCK - 1)
            col = lax.broadcasted_iota(jnp.int32, scores.shape, 1)
            allowed = (col <= row) & (col >= (row & (BLOCK - PATCHES)))
            scores = jnp.where(allowed, scores, masked_score)
            e = jnp.exp(scores - jnp.max(scores, axis=-1, keepdims=True))
            probs = e / jnp.sum(e, axis=-1, keepdims=True)
            pb[layer, b] = probs
            ct[layer, at, :] = gather(mm(probs.astype(bf16), v)).astype(bf16)

    def attention_back(layer, h):
        for b in blocks_of(h):
            at = pl.ds(b * BLOCK, BLOCK)
            spread_d = spread(mm_t(mb[at, :], wb[layer, 960:1280, :]).astype(bf16))
            spread_q = spread(qb[layer, 0, at, :])
            k = qb[layer, 1, at, :]
            v = qb[layer, 2, at, :]
            probs = pb[layer, b]
            d_probs = mm_t(spread_d, v)
            d_scores = (
                probs * (d_probs - jnp.sum(probs * d_probs, axis=-1, keepdims=True))
            ).astype(bf16)
            d_q = gather(mm(d_scores, k)) * inv
            d_k = tm(d_scores, spread_q) * inv
            dqb[0, at, :] = turned(d_q, -1).astype(bf16)
            dqb[1, at, :] = turned(d_k, -1).astype(bf16)
            dqb[2, at, :] = tm(probs.astype(bf16), spread_d).astype(bf16)

    contexts = pl.ds(pl.multiple_of(s * PATCHES, PATCHES), PATCHES)
    flags = missing_ref[contexts, :].astype(f32)
    values = series_ref[contexts, :] * (1.0 - flags)
    for j in range(PATCHES):
        at = pl.ds(j, PATCHES, stride=PATCHES)
        own_points = slice(j * PATCH, (j + 1) * PATCH)
        gpad[at, :] = jnp.concatenate(
            [values[:, own_points], flags[:, own_points], jnp.zeros((PATCHES, 64), f32)], axis=1
        )
    patch_ref[...] = gpad[:, 0:64].astype(bf16)
    for copy in small_inputs:
        copy.wait()
    for h in range(HALVES):
        at = rows_of(h)
        before = mm(patch_ref[at, :], w_in_ref[...])
        pre[at, :] = before
        tokh[at, :] = (before * jax.nn.sigmoid(before)).astype(bf16)
        rs_send(0, h, lambda j, cols: mm(tokh[at, :], w_hid_ref[:, cols]))
    gn_send.wait_recv()
    pltpu.make_async_copy(wb.at[s], wb.at[s], w_loc).wait()
    for h in range(HALVES):
        start_weights(4 + 2 * h, 6 + 2 * h)
        weights(0, [("y", 0)] if h == 0 else [("y", 1), ("y", 2)])
        stream = rs_take(0, h) + mm(patch_ref[chunk(h, z), :], w_res_ref[...])
        sx[0, own(h), :] = stream
        ag_send(0, h, nb.at[0], norm(stream, gn[0, 0:1, :]))
    start_weights(8, 10)
    weights(0, [("x", 0), ("y", 3), ("x", 1), ("x", 2), ("y", 4)])
    weights(1, [("y", 0), ("y", 1), ("y", 2)])

    def lo_rows(sec, h):
        return lo_ref.at[pl.ds(pl.multiple_of(sec * ROWS + h * RH + z * RQ, RQ), RQ)]

    def lo_keep(h):
        return pltpu.make_async_copy(ob.at[s, own(h)], lo_rows(s, h), lo_l.at[h])

    def lo_cross(h):
        return remote(ob.at[other, own(h)], lo_rows(s, h), lo_s.at[0, h], lo_r.at[0, h], y_a)

    def lo_arrive(h):
        return remote(ob.at[other, own(h)], lo_rows(other, h), lo_s.at[0, h], lo_r.at[0, h], y_a)

    def lo_own(h, d):
        return remote(ob.at[s, own(h)], lo_rows(s, h), lo_s.at[1, h], lo_r.at[1, h], z_peer[d])

    def lo_pass(h, d):
        ref = lo_rows(other, h)
        return remote(ref, ref, lo_s.at[2, h], lo_r.at[2, h], z_peer[d])

    def lo_total(i, h):
        ref = pd.at[pl.ds(0, 3 * RQ)]
        return remote(ref, ref, lo_s.at[i, h], lo_r.at[i, h], core)

    def cross_out(layer, h):
        @pl.when(s != layer)
        def _():
            lo_cross(h).start()

    def own_out(h):
        lo_keep(h).start()
        for d in (2, 1, 3):
            lo_own(h, d).start()

    def pass_out(h):
        lo_arrive(h).wait_recv()
        for d in (2, 1, 3):
            lo_pass(h, d).start()

    def mlp_out(layer, h):
        out = (mid[layer, own(h), :] + rs_take(2 + 2 * layer, h)).astype(bf16)
        ob[layer, own(h), :] = out
        cross_out(layer, h)
        return out

    for layer in range(2):
        for h in range(HALVES):
            ag_wait(2 * layer, h, nb.at[layer])
            attention_front(layer, h)
            if h == 0 and layer == 0:
                start_weights(10, 12)
                weights(0, [("y", 5), ("x", 3), ("x", 4), ("y", 6), ("core", 3)])
                weights(1, [("y", 3), ("y", 4), ("y", 5)])
            if h == 0 and layer == 1:
                weights(1, [("core", 3)])
            if h == 1 and layer == 0:
                weights(0, [("y", 7)])
            at = rows_of(h)
            rs_send(
                1 + 2 * layer, h, lambda j, cols: mm(ct[layer, at, :], wb[layer, 960:1280, cols])
            )
        if layer == 0:
            weights(0, [("y", 8), ("x", 5), ("x", 6)])
            weights(1, [("y", 6), ("x", 0), ("x", 1), ("x", 2), ("x", 3)])
        for h in range(HALVES):
            if layer == 0 and h == 1:
                weights(0, [("y", 9), ("x", 7), ("y", 10), ("y", 11)])
                weights(1, [("y", 7)])
            middle = sx[layer, own(h), :] + rs_take(1 + 2 * layer, h)
            mid[layer, own(h), :] = middle
            ag_send(1 + 2 * layer, h, nm.at[layer], norm(middle, gn[layer, 1:2, :]))
        if layer == 0:
            weights(0, [("x", 8)] + [("core", i) for i in range(4, 8)])
            weights(1, [("y", 8), ("y", 9), ("x", 4), ("x", 5)])
        else:
            weights(1, [("core", i) for i in range(4, 8)])
        for h in range(HALVES):
            ag_wait(1 + 2 * layer, h, nm.at[layer])
            at = rows_of(h)

            def up_tile(j, carry):
                cols = cols_of(j)
                up = mm(nm[layer, at, :], wb[layer, 1280:2560, cols])
                upb[layer, at, cols] = up
                t = jnp.tanh(GELU_A * (up + GELU_B * up * up * up))
                hb[at, cols] = (0.5 * up * (1.0 + t)).astype(bf16)

            unrolled(D // TILE, up_tile)
            if layer == 1:
                continue
            if h == 0 and layer == 0:
                weights(0, [("x", 9), ("x", 10), ("x", 11)] + [("core", i) for i in range(8, 12)])
                weights(1, [("y", 10), ("y", 11), ("x", 6), ("x", 7)])
            rs_send(
                2 + 2 * layer, h, lambda j, cols: mm(hb[at, :], wb[layer, 2560:3840, cols])
            )
        if layer == 0:
            weights(1, [("x", 8), ("x", 9)])
            for h in range(HALVES):
                out = mlp_out(0, h)
                stream = out.astype(f32)
                sx[1, own(h), :] = stream
                ag_send(2, h, nb.at[1], norm(stream, gn[1, 0:1, :]))
            weights(1, [("x", 10), ("x", 11)])

    xa = x + 1 - 2 * lax.rem(x, 2)
    xb = 3 - x
    to_xa = (s, xa * 4 + 2 * yh + c, z)
    to_xb = (s, xb * 4 + 2 * yh + c, z)
    j1 = lax.rem(lax.div(x + 1, 2), 2)
    j2 = lax.div(x, 2)
    i1 = lax.div(x, 2)
    i2 = lax.rem(x, 2)
    half_at = (64 + 64 * j1, 192 + 64 * i1)
    half_off = (64 + 64 * (1 - j1), 192 + 64 * (1 - i1))
    quarter_at = (half_at[0] + 32 * j2, half_at[1] + 32 * i2)
    quarter_off = (half_at[0] + 32 * (1 - j2), half_at[1] + 32 * (1 - i2))
    first_peer = (to_xa, to_xb)
    second_peer = (to_xb, to_xa)

    class Group:
        def __init__(self, layer, k):
            self.layer, self.k = layer, k
            self.buf = gv if layer == 1 else wb.at[1]
            self.mine = k * 1280 + c * 640
            self.theirs = k * 1280 + (1 - c) * 640
            self.home = s == layer

        def rows(self, at, n):
            return self.buf.at[pl.ds(pl.multiple_of(self.mine + at, 16), n)]

        def result(self, at, n):
            return go_ref.at[pl.ds(pl.multiple_of(self.mine + at, 16), n)]

        def move(self, i, src, dst, peer):
            return remote(src, dst, e_s.at[self.layer, self.k], e_r.at[self.layer, self.k, i], peer)

        def add(self, at, n, sources):
            def body(i, carry):
                here = pl.ds(pl.multiple_of(self.mine + at + i * 16, 16), 16)
                there = pl.ds(pl.multiple_of(i * 16, 16), 16)
                total = self.buf[here, :].astype(f32)
                for source in sources:
                    total = total + source[there, :].astype(f32)
                self.buf[here, :] = total.astype(bf16)
                return carry

            lax.fori_loop(0, n // 16, body, 0)

        def total(self, i, n):
            ref = th.at[self.k, pl.ds(0, n)]
            return self.move(i, ref, ref, core)

        def core(self):
            src = self.buf.at[pl.ds(pl.multiple_of(self.theirs, 16), 640)]
            return self.move(0, src, th.at[self.k], core)

        def first(self, b, hf):
            dst = r1.at[self.k, pl.ds(128 * b + 64 * hf, 64)]
            return self.move(1, self.rows(320 * hf + half_off[b], 64), dst, first_peer[b])

        def second(self, b, hf):
            dst = r2.at[self.k, pl.ds(64 * b + 32 * hf, 32)]
            return self.move(2, self.rows(320 * hf + quarter_off[b], 32), dst, second_peer[b])

        def a_over_y(self, d):
            src = self.rows(320 * lax.div(y_at[d], 2), 64)
            return self.move(3, src, ra1.at[self.k, d - 1], y_peer[d])

        def a_over_x(self, d):
            src = self.rows(320 * yh + 16 * x_at[d], 16)
            return self.move(4, src, ra2.at[self.k, d - 1], x_peer[d])

        def b_over_y(self, d, b):
            src = self.rows(320 * lax.div(y_at[d], 2) + quarter_at[b], 32)
            return self.move(5, src, rb3.at[self.k, d - 1, pl.ds(32 * b, 32)], y_peer[d])

        def a_back_x(self, d):
            at = 320 * yh + 16 * x
            return self.move(6, self.rows(at, 16), self.result(at, 16), x_peer[d])

        def b_back_y(self, b):
            at = 320 * yh + quarter_at[b]
            return self.move(7, self.rows(at, 32), self.result(at, 32), y_peer[2])

        def back_second(self, b, hf):
            ref = self.result(320 * hf + quarter_at[b], 32)
            return self.move(8, ref, ref, second_peer[b])

        def back_first(self, b, hf):
            ref = self.result(320 * hf + half_at[b], 64)
            return self.move(9, ref, ref, first_peer[b])

        def a_back_y(self):
            ref = self.result(320 * yh, 64)
            return self.move(10, ref, ref, y_peer[2])

        def back_core(self, at, n=640):
            ref = self.result(at, n)
            return self.move(11, ref, ref, core)

        def keep(self, at, n):
            return pltpu.make_async_copy(
                self.rows(at, n), self.result(at, n), e_l.at[self.layer, self.k]
            )

        def to_homes(self, copies):
            @pl.when(self.home)
            def _():
                for copy in copies(2):
                    copy.start()

            @pl.when(jnp.logical_not(self.home))
            def _():
                for d in (1, 3):
                    for copy in copies(d):
                        copy.start()

        def s0(self):
            if self.layer == 0:
                pl.semaphore_wait(free_th.at[self.k], 1)
            self.core().start()

        def s1(self):
            self.core().wait_recv()
            self.add(0, 640, [th.at[self.k]])
            if self.layer == 1:
                pl.semaphore_signal(free_th.at[self.k], inc=1, device_id=core, device_id_type=MESH)
            else:
                pl.semaphore_wait(free_r1.at[self.k], 2)
            for b in range(2):
                for hf in range(2):
                    self.first(b, hf).start()
            self.to_homes(lambda d: [self.a_over_y(d)])

        def s2(self):
            self.total(1, 256).wait_recv()
            for b in range(2):
                for hf in range(2):
                    self.add(
                        320 * hf + half_at[b], 64, [r1.at[self.k, pl.ds(128 * b + 64 * hf, 64)]]
                    )
            if self.layer == 1:
                for peer in (to_xa, to_xb):
                    pl.semaphore_signal(
                        free_r1.at[self.k], inc=1, device_id=peer, device_id_type=MESH
                    )
            else:
                pl.semaphore_wait(free_r2.at[self.k], 2)
            for b in range(2):
                for hf in range(2):
                    self.second(b, hf).start()

        def s3(self):
            self.total(2, 128).wait_recv()
            for b in range(2):
                for hf in range(2):
                    self.add(
                        320 * hf + quarter_at[b], 32, [r2.at[self.k, pl.ds(64 * b + 32 * hf, 32)]]
                    )
            if self.layer == 1:
                for peer in (to_xa, to_xb):
                    pl.semaphore_signal(
                        free_r2.at[self.k], inc=1, device_id=peer, device_id_type=MESH
                    )
            self.to_homes(lambda d: [self.b_over_y(d, b) for b in range(2)])

            @pl.when(self.home)
            def _():
                self.total(3, 192).wait_recv()
                self.add(320 * yh, 64, [ra1.at[self.k, i] for i in range(3)])
                for d in (2, 1, 3):
                    self.a_over_x(d).start()

        def s4(self):
            @pl.when(self.home)
            def _():
                self.total(5, 192).wait_recv()
                for b in range(2):
                    at = 320 * yh + quarter_at[b]
                    self.add(at, 32, [rb3.at[self.k, i, pl.ds(32 * b, 32)] for i in range(3)])
                    self.keep(at, 32).start()
                    self.b_back_y(b).start()
                self.total(4, 48).wait_recv()
                at = 320 * yh + 16 * x
                self.add(at, 16, [ra2.at[self.k, i] for i in range(3)])
                self.keep(at, 16).start()
                for d in (2, 1, 3):
                    self.a_back_x(d).start()

        def s5(self):
            @pl.when(self.home)
            def _():
                self.keep(0, 80).wait()
                self.total(7, 64).wait_recv()
                for b in range(2):
                    for hf in range(2):
                        self.back_second(b, hf).start()
                self.total(6, 48).wait_recv()
                self.a_back_y().start()

        def s6(self):
            @pl.when(self.home)
            def _():
                self.total(8, 128).wait_recv()
                for b in range(2):
                    for hf in range(2):
                        self.back_first(b, hf).start()
                for b in range(2):
                    for hf in range(2):
                        self.back_core(320 * hf + half_at[b], 64).start()

        def s7(self):
            @pl.when(self.home)
            def _():
                self.a_back_y().wait_recv()
                for hf in range(2):
                    self.back_core(320 * hf, 64).start()
                self.total(9, 256).wait_recv()
                for b in range(2):
                    for hf in range(2):
                        self.back_core(320 * hf + half_off[b], 64).start()

        def sent(self, n):
            ref = wb.at[0, pl.ds(0, n)]
            return remote(ref, ref, e_s.at[self.layer, self.k], e_r.at[self.layer, self.k, 0], core)

        def drain(self):
            @pl.when(self.home)
            def _():
                self.back_core(0).wait_recv()
                self.sent(1760 + 640).wait_send()

            @pl.when(jnp.logical_not(self.home))
            def _():
                self.sent(1280).wait_send()

    groups = {(layer, k): Group(layer, k) for layer in range(2) for k in range(3)}
    att1, up1, down1 = (groups[1, k] for k in range(3))
    att0, up0, down0 = (groups[0, k] for k in range(3))

    def put(layer, at, value):
        if layer == 1:
            gv[at, :] = value.astype(bf16)
        else:
            wb[1, at, :] = value.astype(bf16)

    def grad_tiles(layer, k, left, right):
        for i in range(D // TILE):
            put(layer, pl.ds(k * 1280 + i * TILE, TILE), tm(left[:, cols_of(i)], right[...]))
        groups[layer, k].s0()

    def t_move(i, src, dst, peer):
        return remote(src, dst, t_s.at[i], t_r.at[i], peer)

    def t_rows(sec, at, n):
        return gt.at[sec, pl.ds(pl.multiple_of(at, 16), n)]

    def t_result(at, n):
        return go_ref.at[pl.ds(pl.multiple_of(LAYER_ROWS + at, 16), n)]

    def t_core(sec):
        return t_move(0, t_rows(sec, 128 * (1 - c), 128), tt.at[sec], core)

    def t_over_x(d, sec):
        src = t_rows(sec, 128 * c + 32 * x_at[d], 32)
        return t_move(1, src, tx.at[d - 1, sec], x_peer[d])

    def t_over_y(d):
        src = t_rows(lax.rem(y_at[d], 2), 128 * c + 32 * x + 16 * lax.div(y_at[d], 2), 16)
        return t_move(2, src, ty.at[d - 1], y_peer[d])

    t_own = 128 * c + 32 * x + 16 * yh

    def t_back_y():
        return t_move(3, t_rows(s, t_own, 16), t_result(t_own, 16), y_peer[2])

    def t_keep():
        return pltpu.make_async_copy(t_rows(s, t_own, 16), t_result(t_own, 16), t_l)

    def t_back_x(d):
        ref = t_result(128 * c + 32 * x, 32)
        return t_move(4, ref, ref, x_peer[d])

    def t_back_core():
        ref = t_result(128 * c, 128)
        return t_move(5, ref, ref, core)

    def t_total(i, n):
        ref = gt.at[0, pl.ds(0, n)]
        return t_move(i, ref, ref, core)

    def t_add(sec, at, n, sources):
        here = pl.ds(pl.multiple_of(at, 16), n)
        total = gt[sec, here, :].astype(f32)
        for source in sources:
            total = total + source[...].astype(f32)
        gt[sec, here, :] = total.astype(bf16)

    def t1():
        t_total(0, 256).wait_recv()
        for sec in range(2):
            for i in range(4):
                t_add(sec, 128 * c + 32 * i, 32, [tt.at[sec, pl.ds(32 * i, 32)]])
            for d in (2, 1, 3):
                t_over_x(d, sec).start()

    def t2():
        t_total(1, 192).wait_recv()
        for sec in range(2):
            t_add(sec, 128 * c + 32 * x, 32, [tx.at[i, sec] for i in range(3)])
        for d in (2, 1, 3):
            t_over_y(d).start()

    def t3():
        t_total(2, 48).wait_recv()
        t_add(s, t_own, 16, [ty.at[i] for i in range(3)])
        t_keep().start()
        t_back_y().start()

    def t4():
        t_keep().wait()
        t_back_y().wait_recv()
        for d in (2, 1, 3):
            t_back_x(d).start()

    def t5():
        t_total(4, 96).wait_recv()
        t_back_core().start()

    weights(1, [("core", i) for i in range(8, 12)])
    cot_copy.wait()
    grad_tiles(1, 2, hb, gb.at[0])
    gg[...] = jnp.zeros_like(gg)

    for layer in (1, 0):
        st = 5 if layer == 1 else 7
        for h in range(HALVES):
            at = rows_of(h)
            if layer == 0:
                ag_wait(5, h, gb.at[1])

            def d_up_tile(j, carry):
                cols = cols_of(j)
                rows = pl.ds(2560 + j * TILE, TILE)
                d_hidden = mm_t(gb[1 - layer, at, :], wb[layer, rows, :])
                up = upb[layer, at, cols]
                t = jnp.tanh(GELU_A * (up + GELU_B * up * up * up))
                slope = 0.5 * (1.0 + t) + 0.5 * up * (1.0 - t * t) * (
                    GELU_A * (1.0 + 3.0 * GELU_B * up * up)
                )
                du[at, cols] = (d_hidden * slope).astype(bf16)
                if layer == 0:
                    hb[at, cols] = (0.5 * up * (1.0 + t)).astype(bf16)

            unrolled(D // TILE, d_up_tile)
            if layer == 0 and h == 1:
                up1.s2()
            if layer == 1 and h == 1:
                down1.s1()
            rs_send(
                st, h,
                lambda j, cols: mm_t(
                    du[at, :], wb[layer, pl.ds(1280 + j * TILE, TILE), :]
                ),
            )
        if layer == 0:
            w_sent(4, x_s, x_r).wait_send()
            w_sent(2, f_s, f_r).wait_send()
        if layer == 0:
            grad_tiles(0, 2, hb, gb.at[1])
        for h in range(HALVES):
            dn = rs_take(st, h)
            dx, gain = norm_back(dn, mid[layer, own(h), :], gn[layer, 1:2, :])
            dm = gb[1 - layer, chunk(h, z), :].astype(f32) + dx
            dmid[own(h), :] = dm
            gg[2 * layer + 1 : 2 * layer + 2, :] += gain
            if layer == 0:
                ag_total(4, h).wait_send()
            ag_send(st - 1, h, mb, dm)
        grad_tiles(layer, 1, nm.at[layer], du)
        if layer == 1:
            for j in range(D // TILE):
                pd[:, cols_of(j)] = mm(hb[...], wb[1, 2560:3840, cols_of(j)]).astype(bf16)
            down1.s2()
        else:
            down0.s1()
        for h in range(HALVES):
            ag_wait(st - 1, h, mb)
            attention_back(layer, h)
            if h == 1 and layer == 1:
                up1.s1()
            if h == 1 and layer == 0:
                up0.s1()
                up1.s3()
                att1.s2()
            at = rows_of(h)
            rs_send(
                st + 1, h,
                lambda j, cols: mm(dqb[0, at, :], wb[layer, 0:ATT, cols])
                + mm(dqb[1, at, :], wb[layer, ATT : 2 * ATT, cols])
                + mm(dqb[2, at, :], wb[layer, 2 * ATT : 3 * ATT, cols]),
            )
        for i in range(3):
            put(layer, pl.ds(i * ATT, ATT), tm(dqb[i], nb[layer]))
        put(layer, pl.ds(960, 320), tm(ct[layer], mb[...]))
        groups[layer, 0].s0()
        if layer == 1:
            down1.s3()
        else:
            down0.s2()
        for h in range(HALVES):
            dn = rs_take(st + 1, h)
            dx, gain = norm_back(dn, sx[layer, own(h), :], gn[layer, 0:1, :])
            gg[2 * layer : 2 * layer + 1, :] += gain
            ag_send(st, h, gb.at[layer], dmid[own(h), :] + dx)
        if layer == 1:
            att1.s1()
        else:
            att0.s1()
            up0.s2()
            down1.s4()

    def gg_copy(d):
        return remote(gg, ggr.at[d - 1], gg_s, gg_r, z_peer[d])

    for d in (1, 2, 3):
        gg_copy(d).start()

    for h in range(HALVES):
        ag_wait(7, h, gb.at[0])
        rs_send(4, h, None)
        at = rows_of(h)
        low = gb[0, at, :]
        before = pre[at, :]
        sig = jax.nn.sigmoid(before)
        d_pre = (
            mm_t(low, w_hid_ref[...]) * (sig * (1.0 + before * (1.0 - sig)))
        ).astype(bf16)
        dctx[at, :] = d_pre
        points = mm_t(d_pre, w_in_ref[...])
        points = points + jnp.where(z == 0, mm_t(low, w_res_ref[...]), 0.0)
        keep = 1.0 - patch_ref[at, :].astype(f32)
        gpad[at, 0:PATCH] = points[:, 0:PATCH] * keep[:, PATCH : 2 * PATCH]
    down0.s3()
    points = gpad[:, 0:64]
    high = points.astype(bf16)
    low = (points - high.astype(f32)).astype(bf16)
    row = lax.broadcasted_iota(jnp.int32, (ROWS, ROWS), 0)
    col = lax.broadcasted_iota(jnp.int32, (ROWS, ROWS), 1)
    swap = jnp.where(
        ((row >> 4) == (col & 15)) & ((row & 15) == (col >> 4)), 1.0, 0.0
    ).astype(bf16)
    points = mm(swap, high) + mm(swap, low)
    for k in range(8):
        dps[k, :, 0:64] = points[k * 32 : (k + 1) * 32]
        dps[k, :, 64:128] = jnp.zeros((32, 64), f32)
    me = s * 4 + z

    def dp_copy(d):
        to = lax.rem(me + d, 8)
        return remote(
            dps.at[to], dpr.at[me], dp_s, dp_r,
            (lax.div(to, 4), dp, lax.rem(to, 4)),
        )

    for d in range(1, 8):
        dp_copy(d).start()
    dpr[me] = dps[me]

    grad_low = gb[0]
    hid = tm(tokh[...], grad_low).astype(bf16)
    res = tm(patch_ref[...], grad_low).astype(bf16)
    inn = tm(patch_ref[...], dctx[...]).astype(bf16)
    for sec in range(2):
        lanes = slice(sec * 640, sec * 640 + 640)
        gt[sec, 0:160, 0:640] = hid[0:160, lanes]
        gt[sec, 0:160, 640:1280] = hid[160:320, lanes]
        gt[sec, 160:192, 0:640] = res[0:32, lanes]
        gt[sec, 160:192, 640:1280] = res[32:64, lanes]
        gt[sec, 192:224, :] = jnp.zeros((32, D), bf16)
        gt[sec, 192:224, 0:320] = inn[sec * 32 : sec * 32 + 32]
    total = gg[...]
    remote(ggr, ggr, gg_s, gg_r, core).wait_recv()
    for d in (1, 2, 3):
        total = total + ggr[d - 1]
    for sec in range(2):
        gt[sec, 224:256, :] = jnp.concatenate(
            [total[2 * sec : 2 * sec + 2], jnp.zeros((30, D), f32)], axis=0
        ).astype(bf16)

    for sec in range(2):
        t_core(sec).start()
    att1.s3()
    att0.s2()
    up0.s3()
    t1()
    down0.s4()
    down1.s5()
    att0.s3()
    up1.s4()
    t2()
    down0.s5()
    up0.s4()
    att1.s4()
    for h in range(HALVES):
        mlp_out(1, h)
        own_out(h)
    down1.s6()
    down0.s6()
    up0.s5()
    up1.s5()
    att0.s4()
    att1.s5()
    t3()
    att0.s5()
    up0.s6()
    up1.s6()
    down0.s7()
    down1.s7()
    t4()
    att0.s6()
    att1.s6()
    up0.s7()
    up1.s7()
    for h in range(HALVES):
        pass_out(h)
    t5()
    att0.s7()
    att1.s7()
    seven = dps.at[pl.ds(0, 7)]
    remote(seven, seven, dp_s, dp_r, core).wait_recv()
    for sec in range(2):
        points_ref[sec] = dpr[4 * sec] + dpr[4 * sec + 1] + dpr[4 * sec + 2] + dpr[4 * sec + 3]

    w_sent(4, w_s, w_r).wait_send()
    for group in groups.values():
        group.drain()
    for i, n in ((0, 256), (1, 192), (2, 48), (3, 16), (4, 96)):
        t_total(i, n).wait_send()
    t_back_core().wait()
    gn_send.wait_send()
    for h in range(HALVES):
        rs_total(7, h).wait_send()
        rs_total(4, h).wait_send()
        for st in (0, 1, 2, 3, 5, 6, 7):
            ag_total(st, h).wait_send()
        lo_cross(h).wait_send()
        lo_keep(h).wait()
        for i in (1, 2):
            lo_total(i, h).wait()
    remote(ggr, ggr, gg_s, gg_r, core).wait_send()
    remote(seven, seven, dp_s, dp_r, core).wait_send()


def run_layers(series, missing, w_in, w_hid, w_res, gain_a, gain_m, wq, wo, wu, wd, cotangent):
    cos, sin, turn = rotary_arrays()
    vm = pl.BlockSpec(memory_space=pltpu.VMEM)
    hbm = pl.BlockSpec(memory_space=pl.ANY)
    dma = pltpu.SemaphoreType.DMA
    scratch = [
        pltpu.VMEM((2 * PATCH, ATT), bf16),
        pltpu.VMEM((ATT, D), bf16),
        pltpu.VMEM((2 * PATCH, D), bf16),
        pltpu.VMEM((BLOCK, ATT), f32),
        pltpu.VMEM((BLOCK, ATT), f32),
        pltpu.VMEM((ATT, ATT), bf16),
        dma((6,)),
        pltpu.VMEM((ROWS, 2 * PATCH), bf16),
        pltpu.VMEM((2, LAYER_ROWS, D), bf16),
        pltpu.VMEM((2, 2, D), f32),
        pltpu.VMEM((ROWS, ATT), bf16),
        pltpu.VMEM((ROWS, ATT), f32),
        pltpu.VMEM((2, ROWS // 4, D), f32),
        pltpu.VMEM((2, ROWS // 4, D), f32),
        pltpu.VMEM((2, ROWS, D), bf16),
        pltpu.VMEM((2, ROWS, D), bf16),
        pltpu.VMEM((2, 3, ROWS, ATT), bf16),
        pltpu.VMEM((2, ROWS // BLOCK, HEADS_HERE * BLOCK, BLOCK), f32),
        pltpu.VMEM((2, ROWS, ATT), bf16),
        pltpu.VMEM((2, ROWS, D), f32),
        pltpu.VMEM((ROWS, D), bf16),
        pltpu.VMEM((2, ROWS, D), bf16),
        pltpu.VMEM((ROWS, D), bf16),
        pltpu.VMEM((ROWS, D), bf16),
        pltpu.VMEM((3, ROWS, ATT), bf16),
        pltpu.VMEM((ROWS, ATT), bf16),
        pltpu.VMEM((LAYER_ROWS, D), bf16),
        pltpu.VMEM((2, PACK_ROWS - LAYER_ROWS, D), bf16),
        pltpu.VMEM((2, ROWS, D), bf16),
        pltpu.VMEM((2, 3, ROWS // 4, D), bf16),
        pltpu.VMEM((ROWS // 4, D), f32),
        pltpu.VMEM((2, ROWS // 4, D), bf16),
        pltpu.VMEM((8, D), f32),
        pltpu.VMEM((3, 8, D), f32),
        pltpu.VMEM((8, 32, 128), f32),
        pltpu.VMEM((8, 32, 128), f32),
        pltpu.VMEM((ROWS, 128), f32),
        pltpu.VMEM((3, 640, D), bf16),
        pltpu.VMEM((3, 256, D), bf16),
        pltpu.VMEM((3, 128, D), bf16),
        pltpu.VMEM((3, 3, 64, D), bf16),
        pltpu.VMEM((3, 3, 16, D), bf16),
        pltpu.VMEM((3, 3, 64, D), bf16),
        pltpu.VMEM((2, 128, D), bf16),
        pltpu.VMEM((3, 2, 32, D), bf16),
        pltpu.VMEM((3, 16, D), bf16),
        pltpu.VMEM((ROWS, D), bf16),
        dma, *[dma, dma((N_PIECES,))] * 3,
        dma, dma, dma,
        dma((9, HALVES)), dma((9, HALVES)),
        dma((8, HALVES)), dma((8, HALVES)),
        dma((HALVES,)), dma((3, HALVES)), dma((3, HALVES)),
        dma, dma, dma, dma,
        dma((2, 3)), dma((2, 3, 12)), dma((2, 3)),
        dma((6,)), dma((6,)), dma,
        *[pltpu.SemaphoreType.REGULAR((3,))] * 3,
    ]
    return pl.pallas_call(
        layers_kernel,
        out_shape=(
            jax.ShapeDtypeStruct((2 * ROWS, D), bf16),
            jax.ShapeDtypeStruct((PACK_ROWS, D), bf16),
            jax.ShapeDtypeStruct((2, 32, 128), f32),
        ),
        in_specs=[vm] * 2 + [hbm] * 3 + [vm] * 2 + [hbm] * 8,
        out_specs=(hbm, hbm, vm),
        scratch_shapes=scratch,
        compiler_params=pltpu.CompilerParams(
            collective_id=0, has_side_effects=True, vmem_limit_bytes=62 * 2**20
        ),
        cost_estimate=pl.CostEstimate(
            flops=15_000_000_000, bytes_accessed=50_000_000, transcendentals=4_000_000
        ),
        name="layers",
    )(
        series, missing, w_in, w_hid, w_res, gain_a, gain_m, wq, wo, wu, wd, cotangent,
        jnp.asarray(cos, f32), jnp.asarray(sin, f32), jnp.asarray(turn, bf16),
    )


STEP = 320
STEPS = LAYER_ROWS // STEP


def widen_kernel(
    total_ref, lo_ref, points_ref,
    qkv, out, up, down, hid, res, inn, gain_a, gain_m, series_grad, lo_out,
    low, wide, small, kept, in_sem, out_sem, small_sem, lo_sem,
):
    places_of = [(qkv, i) for i in range(3)] + [(out, 0)]
    places_of += [(up, i) for i in range(4)] + [(down, i) for i in range(4)]

    def rows(i):
        return pl.ds(i * STEP, STEP)

    def load(i):
        return pltpu.make_async_copy(total_ref.at[rows(i)], low.at[rows(i)], in_sem.at[i])

    def store(i):
        ref, k = places_of[i]
        return pltpu.make_async_copy(wide.at[rows(i)], ref.at[rows(k)], out_sem.at[i])

    load_small = pltpu.make_async_copy(
        total_ref.at[pl.ds(LAYER_ROWS, PACK_ROWS - LAYER_ROWS)], small, small_sem
    )
    load_lo = pltpu.make_async_copy(lo_ref, kept, lo_sem)
    store_lo = pltpu.make_async_copy(kept, lo_out, lo_sem)
    for i in range(STEPS):
        load(i).start()
    load_small.start()
    load_lo.start()
    for i in range(STEPS):
        load(i).wait()

        def body(j, carry, i=i):
            at = pl.ds(pl.multiple_of(i * STEP + j * 32, 32), 32)
            wide[at, :] = low[at, :].astype(f32)
            return carry

        lax.fori_loop(0, STEP // 32, body, 0, unroll=2)
        store(i).start()
    load_lo.wait()
    store_lo.start()
    load_small.wait()
    values = small[...].astype(f32)
    hid[0:160, :] = values[0:160, 0:640]
    hid[160:320, :] = values[0:160, 640:1280]
    res[0:32, :] = values[160:192, 0:640]
    res[32:64, :] = values[160:192, 640:1280]
    inn[...] = values[192:224, 0:320]
    gain_a[...] = values[224:225]
    gain_m[...] = values[225:226]
    for sec in range(2):
        for j in range(2):
            series_grad[16 * sec : 16 * sec + 16, 32 * j : 32 * j + 32] = points_ref[
                sec, 16 * j : 16 * j + 16, 0:32
            ]
    for i in range(STEPS):
        store(i).wait()
    store_lo.wait()


def widen(total, layer_out, points):
    shapes = ((960, D), (320, D), (1280, D), (1280, D), (320, 640), (64, 640), (32, 320), (1, D), (1, D), (32, 64))
    hbm = pl.BlockSpec(memory_space=pl.ANY)
    vm = pl.BlockSpec(memory_space=pltpu.VMEM)
    dma = pltpu.SemaphoreType.DMA
    return pl.pallas_call(
        widen_kernel,
        out_shape=[jax.ShapeDtypeStruct(shape, f32) for shape in shapes]
        + [jax.ShapeDtypeStruct((2 * ROWS, D), bf16)],
        in_specs=[hbm, hbm, vm],
        out_specs=[hbm] * 4 + [vm] * 6 + [hbm],
        scratch_shapes=[
            pltpu.VMEM((LAYER_ROWS, D), bf16),
            pltpu.VMEM((LAYER_ROWS, D), f32),
            pltpu.VMEM((PACK_ROWS - LAYER_ROWS, D), bf16),
            pltpu.VMEM((2 * ROWS, D), bf16),
            dma((STEPS,)), dma((STEPS,)), dma, dma,
        ],
        compiler_params=pltpu.CompilerParams(vmem_limit_bytes=60 * 2**20),
        cost_estimate=pl.CostEstimate(flops=0, bytes_accessed=32_000_000, transcendentals=0),
        name="widen",
    )(total, layer_out, points)


def per_device(
    series, missing, w_in, w_hid, w_res, gain_attn, w_qkv, w_out, gain_mlp, w_up, w_down, cotangent
):
    wq = jnp.transpose(w_qkv[0], (1, 2, 0)).reshape(3 * ATT, D)
    layer_out, total, points = run_layers(
        series, missing, w_in, w_hid, w_res, gain_attn, gain_mlp, wq, w_out[0], w_up[0], w_down[0],
        cotangent,
    )
    g_qkv, g_out, g_up, g_down, g_hid, g_res, g_in, gain_a, gain_m, series_grad, layer_out = widen(
        total, layer_out, points
    )
    g_qkv = jnp.transpose(g_qkv.reshape(3, ATT, D), (2, 0, 1))
    return (
        layer_out[None],
        series_grad,
        g_in,
        g_hid,
        g_res,
        gain_a,
        g_qkv[None],
        g_out[None],
        gain_m,
        g_up[None],
        g_down[None],
    )


def solution(mesh):
    in_specs = (
        P("dp", None),
        P("dp", None),
        P(None, "tensor"),
        P("tensor", None),
        P(),
        P("section", None),
        P("section", None, None, "tensor"),
        P("section", "tensor", None),
        P("section", None),
        P("section", None, "tensor"),
        P("section", "tensor", None),
        P("dp", None),
    )
    out_specs = (
        P("section", "dp", None),
        P("dp", ("section", "tensor")),
        P("section", "tensor"),
        P("tensor", "section"),
        P(None, "section"),
        P("section", None),
        P("section", None, None, "tensor"),
        P("section", "tensor", None),
        P("section", None),
        P("section", None, "tensor"),
        P("section", "tensor", None),
    )
    return jax.shard_map(
        per_device, mesh=mesh, in_specs=in_specs, out_specs=out_specs, check_vma=False
    )
```

profile of v0, /device:TPU:1, one launch (start us, length us, event | category | flops | bytes accessed | tf_op | source)
XLA Modules:
  0.0 235.4 jit_solution(16179868789135647863)
XLA Ops:
  0.6 221.7 %layers.1 = (bf16[512,1280]{1,0:T(8,128)(2,1)}, bf16[4096,1280]{1,0:T(8,128)(2,1)}, f32[2,32,128]{2,1,0:T(8,128)}) custom-call(f32[32,512]{1,0:T(8,128)} %series_ref.1, s32[32,512]{1,0:T(8,128)} %missing_ref.1, bf16[64,320]{1,0:T(8,128)(2,1)} %w_in_in.1, bf16[320,1280]{1,0:T(8,128)(2,1)} %w_hid_in.1, bf16[64,1280]{1,0:T(8,128)(2,1)} %w_res_in.1, ...), custom_call_target="tpu_custom_call" | custom-call | flops 15000000512 | bytes 50000000 | tf_op jit(solution)/shard_map/layers/pallas_call | solution.py:1105
  222.4 12.5 %widen.1 = (f32[960,1280]{1,0:T(8,128)}, f32[320,1280]{1,0:T(8,128)}, f32[1280,1280]{1,0:T(8,128)}, f32[1280,1280]{1,0:T(8,128)}, f32[320,640]{1,0:T(8,128)}, /*...) custom-call(bf16[4096,1280]{1,0:T(8,128)(2,1)} %get-tuple-element.25, ...), custom_call_target="tpu_custom_call" | custom-call | bytes 32000000 | tf_op jit(solution)/shard_map/widen/pallas_call | solution.py:1195
where the time goes:
time: 239 us; the launch traced here: 235 us
  Pallas kernels  234 us (98%)
    pallas_call x1, Pallas kernels, run_layers(): pl.pallas_call(layers_kernel, out_shape=(jax.ShapeDtypeStruct((2 * ROWS,...  222 us
    pallas_call x1, Pallas kernels, widen(): pl.pallas_call(widen_kernel, out_shape=[jax.ShapeDtypeStruct(shape, f32)...  12.5 us

commit v1 on v0

--- a/solution.py
+++ b/solution.py
@@ -235,8 +235,8 @@
         def body(j, carry):
             cols = cols_of(j)
             sb[st % 2, rows_of(h), cols] = produce(j, cols).astype(bf16)
-            if j in (2, 4):
-                part = pl.ds(0, 768) if j == 2 else pl.ds(768, 512)
+            if j in (1, 3, 4):
+                part = {1: pl.ds(0, 512), 3: pl.ds(512, 512), 4: pl.ds(1024, 256)}[j]
                 for d in (2, 1, 3):
                     rs_copy(st, h, d, part).start()
 
@@ -522,16 +522,18 @@
             return remote(src, dst, e_s.at[self.layer, self.k], e_r.at[self.layer, self.k, i], peer)
 
         def add(self, at, n, sources):
+            step = 32 if n % 32 == 0 and len(sources) == 1 else 16
+
             def body(i, carry):
-                here = pl.ds(pl.multiple_of(self.mine + at + i * 16, 16), 16)
-                there = pl.ds(pl.multiple_of(i * 16, 16), 16)
+                here = pl.ds(pl.multiple_of(self.mine + at + i * step, 16), step)
+                there = pl.ds(pl.multiple_of(i * step, 16), step)
                 total = self.buf[here, :].astype(f32)
                 for source in sources:
                     total = total + source[there, :].astype(f32)
                 self.buf[here, :] = total.astype(bf16)
                 return carry
 
-            lax.fori_loop(0, n // 16, body, 0)
+            lax.fori_loop(0, n // step, body, 0)
 
         def total(self, i, n):
             ref = th.at[self.k, pl.ds(0, n)]
@@ -1002,6 +1004,8 @@
     att0.s5()
     up0.s6()
     up1.s6()
+    for h in range(HALVES):
+        pass_out(h)
     down0.s7()
     down1.s7()
     t4()
@@ -1009,8 +1013,6 @@
     att1.s6()
     up0.s7()
     up1.s7()
-    for h in range(HALVES):
-        pass_out(h)
     t5()
     att0.s7()
     att1.s7()

time: 239 us -> 237 us (level)
  Pallas kernels: 234 us -> 231 us
    pallas_call x1, Pallas kernels: 222 us -> 219 us  [run_layers(): pl.pallas_call(layers_kernel, out_shape=(jax.ShapeDtypeStruct((2 * ROWS,...]
where the time goes in v1:
time: 237 us; the launch traced here: 232 us
  Pallas kernels  231 us (97%)
    pallas_call x1, Pallas kernels, run_layers(): pl.pallas_call(layers_kernel, out_shape=(jax.ShapeDtypeStruct((2 * ROWS,...  219 us
    pallas_call x1, Pallas kernels, widen(): pl.pallas_call(widen_kernel, out_shape=[jax.ShapeDtypeStruct(shape, f32)...  12.5 us

profile of v1, /device:TPU:1, one launch (start us, length us, event | category | flops | bytes accessed | tf_op | source)
XLA Modules:
  0.0 232.3 jit_solution(17327475635275858224)
XLA Ops:
  0.6 218.6 %layers.1 = (bf16[512,1280]{1,0:T(8,128)(2,1)}, bf16[4096,1280]{1,0:T(8,128)(2,1)}, f32[2,32,128]{2,1,0:T(8,128)}) custom-call(f32[32,512]{1,0:T(8,128)} %series_ref.1, s32[32,512]{1,0:T(8,128)} %missing_ref.1, bf16[64,320]{1,0:T(8,128)(2,1)} %w_in_in.1, bf16[320,1280]{1,0:T(8,128)(2,1)} %w_hid_in.1, bf16[64,1280]{1,0:T(8,128)(2,1)} %w_res_in.1, ...), custom_call_target="tpu_custom_call" | custom-call | flops 15000000512 | bytes 50000000 | tf_op jit(solution)/shard_map/layers/pallas_call | solution.py:1107
  219.2 12.5 %widen.1 = (f32[960,1280]{1,0:T(8,128)}, f32[320,1280]{1,0:T(8,128)}, f32[1280,1280]{1,0:T(8,128)}, f32[1280,1280]{1,0:T(8,128)}, f32[320,640]{1,0:T(8,128)}, /*...) custom-call(bf16[4096,1280]{1,0:T(8,128)(2,1)} %get-tuple-element.25, ...), custom_call_target="tpu_custom_call" | custom-call | bytes 32000000 | tf_op jit(solution)/shard_map/widen/pallas_call | solution.py:1197
